TPU v7x, 32 devices: a whole 2x2x4 slice. The times are simulated.
32 devices in a mesh: groups: 2 (over y), dom: 8 (over z, x), event: 2 (over core).
Axes of the slice: x: 2, y: 2, z: 4, core: 2. Of those that a mesh axis runs over, the one named last changes fastest.
Arguments:
- wavefields: float32 [8, 12, 65536], P(('groups', 'event'), None, 'dom'), parts along dimension 0, may hold values from -6 to 6
- element_nodes: int32 [125, 1024], P(None, 'dom'), may hold values from 0 to 8191, as said below
- inverse_jacobian: float32 [9, 1024], P(None, 'dom'), may hold values from -0.45 to 1.6
- jacobian_det: float32 [1024], P('dom'), may hold values from 0.5 to 2
- moduli: float32 [2, 125, 1024], P(None, None, 'dom'), may hold values from 0.3 to 3
- inverse_mass: float32 [65536], P('dom'), may hold values from 0.02 to 0.06
- neighbours: int32 [8, 6], replicated, may hold values from 0 to 7, as said below
- shared_counts: int32 [8, 6], P('dom'), may hold values from 1 to 192, as said below
- shared_points: int32 [8, 6, 192], P('dom'), may hold values from 0 to 1023, as said below
Outputs:
- next_wavefields: float32 [8, 12, 65536], P(('groups', 'event'), None, 'dom'), parts along dimension 0
- sensitivity: float32 [4, 125, 1024], P('groups', None, ('dom', 'event')), parts along dimension 0
There are 2 independent parts, one for each index of `groups`. A program takes and returns all parts, laid end to end along the dimension named above; an argument that names none is the same for every part. Nothing has to cross between parts.
Inputs may be any that keep to these rules, and one draw needn't show every extreme that they name: `neighbours`: each row lists 6 distinct partitions other than its own; if p lists d then d lists p. `shared_counts`: the count of d's slot naming p equals that of p's slot naming d; one count equals 192 in every draw. `shared_points`: entries at or past the slot's count are unused. `element_nodes`: elements 32 and later of each partition touch only points 1024 and above.
All inputs are finite; a program needn't handle non-finite values.
Results may differ from a plain program's by a relative error of at most 0.0001.
Values sent between devices are 32-bit elements; how exact they have to be, the bound alone decides.
A program may use at most 64 MiB of HBM per device.

v0:
```python
import jax
import jax.numpy as jnp
import numpy as np
from jax import lax
from jax.experimental import pallas as pl
from jax.experimental.pallas import tpu as pltpu
from jax.sharding import PartitionSpec as P

STEPS = 2
WIDE = 256
NOWHERE = 1 << 24

time_step = 0.5
kernel_weight = 0.01
highest = lax.Precision.HIGHEST
f32 = jnp.float32
bf16 = jnp.bfloat16


def node_tables():
    points = np.array([-1.0, -np.sqrt(3.0 / 7.0), 0.0, np.sqrt(3.0 / 7.0), 1.0])
    legendre = (35.0 * points**4 - 30.0 * points**2 + 3.0) / 8.0
    derivative = np.zeros((5, 5))
    for a in range(5):
        for b in range(5):
            if a != b:
                derivative[a, b] = legendre[a] / (legendre[b] * (points[a] - points[b]))
    derivative[0, 0] = -5.0
    derivative[4, 4] = 5.0
    weights = np.array([0.1, 49.0 / 90.0, 32.0 / 45.0, 49.0 / 90.0, 0.1])
    cube_weights = weights[:, None, None] * weights[None, :, None] * weights[None, None, :]
    return (derivative, cube_weights)


def padded_tables():
    derivative, cube = node_tables()
    eye = np.eye(5)
    along = (
        np.kron(eye, np.kron(eye, derivative)),
        np.kron(eye, np.kron(derivative, eye)),
        np.kron(derivative, np.kron(eye, eye)),
    )
    forward = np.zeros((3 * 128, 128), np.float32)
    backward = np.zeros((128, 3 * 128), np.float32)
    for d in range(3):
        forward[d * 128 : d * 128 + 125, :125] = along[d]
        backward[:125, d * 128 : d * 128 + 125] = along[d].T
    volume = np.zeros((128, 128), np.float32)
    volume[:125] = cube.reshape(125, 1)
    return forward, backward, volume


def split(values):
    upper = values.astype(bf16)
    lower = (values - upper.astype(f32)).astype(bf16)
    return upper, lower


def columns_onehot(column_ids):
    rows = lax.broadcasted_iota(jnp.int32, (WIDE, column_ids.shape[1]), 0)
    return jnp.where(rows == column_ids, 1.0, 0.0).astype(bf16)


def pick_rows(result, row_ids, group):
    mask = lax.broadcasted_iota(jnp.int32, (group, 128), 0) == row_ids
    return [
        jnp.sum(
            jnp.where(mask, result[c * group : (c + 1) * group], 0.0), axis=0, keepdims=True
        )
        for c in range(12)
    ]


def slot_onehot(slots_ref):
    return jnp.concatenate(
        [columns_onehot(slots_ref[r : r + 1, :] & (WIDE - 1)) for r in range(12)], axis=1
    )


def combine(present_ref, earlier_ref, force_ref, arrived_ref, mass_ref, slots_ref, peers_ref, following_ref):
    domains = arrived_ref.shape[0]
    rows = mass_ref.shape[0]
    blocks = []
    for k in range(6):
        block = jnp.zeros((12, WIDE), f32)
        for p in range(domains):
            block = jnp.where(peers_ref[0, k] == p, arrived_ref[p], block)
        blocks.append(block)
    received = jnp.concatenate(blocks, axis=1)
    onehot = slot_onehot(slots_ref)
    pieces = []
    for r in range(12):
        mask = lax.broadcasted_iota(jnp.int32, (8, 128), 0) == (slots_ref[r : r + 1, :] >> 8)
        part = received[:, r * 128 : (r + 1) * 128]
        pieces.append(
            jnp.concatenate(
                [jnp.where(mask, part[c : c + 1, :], 0.0) for c in range(12)], axis=0
            )
        )
    spread = jnp.concatenate(pieces, axis=1)
    upper, lower = split(spread)
    both = lax.dot_general(
        jnp.concatenate([upper, lower], axis=0), onehot, (((1,), (1,)), ((), ())),
        preferred_element_type=f32,
    )
    added = both[:96] + both[96:]
    mass = mass_ref[...] * (time_step * time_step)
    for c in range(12):
        where = slice(c * rows, (c + 1) * rows)
        force = force_ref[where, :]
        total = jnp.concatenate([force[:8] + added[c * 8 : (c + 1) * 8], force[8:]], axis=0)
        following_ref[where, :] = 2.0 * present_ref[where, :] - earlier_ref[where, :] - mass * total


def forces(
    present_ref, ids_ref, jacobian_ref, det_ref, moduli_ref, slots_ref, peers_ref,
    forward_ref, backward_ref, volume_ref,
    force_ref, sending_ref, terms_ref,
    onehot_ref, nodal_ref, along_ref, traction_ref, nodal_force_ref, sum_ref,
):
    rows = present_ref.shape[0] // 12
    upper, lower = split(present_ref[...])
    table = jnp.concatenate([upper, lower], axis=1)
    sublane = lax.broadcasted_iota(jnp.int32, (8, 128), 0)

    def gather(g, carry):
        base = pl.multiple_of(g * 8, 8)
        ids = ids_ref[pl.ds(base, 8), :]
        onehot = jnp.concatenate(
            [columns_onehot((ids & (WIDE - 1))[r : r + 1, :]) for r in range(8)], axis=1
        )
        onehot_ref[g] = onehot
        result = jnp.dot(
            table, jnp.concatenate([onehot, onehot], axis=0), preferred_element_type=f32
        )
        row_ids = ids >> 8
        gathered = [jnp.zeros((8, 128), f32)] * 12
        for r in range(8):
            picked = pick_rows(result[:, r * 128 : (r + 1) * 128], row_ids[r : r + 1, :], rows)
            gathered = [jnp.where(sublane == r, picked[c], gathered[c]) for c in range(12)]
        nodal_ref[pl.ds(base, 8), :] = jnp.concatenate(gathered, axis=1)
        return carry

    lax.fori_loop(0, 16, gather, 0)
    along_ref[...] = jnp.dot(
        forward_ref[...], nodal_ref[...], precision=highest, preferred_element_type=f32
    )

    def elements(g, carry):
        base = pl.multiple_of(g * 8, 8)
        jac = [jnp.broadcast_to(jacobian_ref[i : i + 1, :], (8, 128)) for i in range(9)]
        shear = moduli_ref[0, pl.ds(base, 8), :]
        bulk = moduli_ref[1, pl.ds(base, 8), :]
        lame = bulk - 2.0 / 3.0 * shear
        volume = volume_ref[pl.ds(base, 8), :] * det_ref[...]
        scaled = [volume * jac[i] for i in range(9)]
        shear_sum = jnp.zeros((8, 128), f32)
        bulk_sum = jnp.zeros((8, 128), f32)
        for event in range(2):
            kept = []
            for field in range(2):
                first = (event * 2 + field) * 3
                local = [
                    [
                        along_ref[pl.ds(d * 128 + base, 8), (first + c) * 128 : (first + c + 1) * 128]
                        for c in range(3)
                    ]
                    for d in range(3)
                ]
                grad = [
                    [
                        local[0][c] * jac[m] + local[1][c] * jac[3 + m] + local[2][c] * jac[6 + m]
                        for c in range(3)
                    ]
                    for m in range(3)
                ]
                div = grad[0][0] + grad[1][1] + grad[2][2]
                strain = {}
                stress = {}
                deviator = {}
                for c in range(3):
                    for m in range(c, 3):
                        if c == m:
                            strain[c, m] = grad[c][c]
                            deviator[c, m] = strain[c, m] - div * (1.0 / 3.0)
                            stress[c, m] = 2.0 * shear * strain[c, m] + lame * div
                        else:
                            twice = grad[m][c] + grad[c][m]
                            strain[c, m] = 0.5 * twice
                            deviator[c, m] = strain[c, m]
                            stress[c, m] = shear * twice
                            stress[m, c] = stress[c, m]
                kept.append((deviator, div))
                for c in range(3):
                    for d in range(3):
                        traction_ref[
                            pl.ds(d * 128 + base, 8), (first + c) * 128 : (first + c + 1) * 128
                        ] = (
                            stress[c, 0] * scaled[3 * d]
                            + stress[c, 1] * scaled[3 * d + 1]
                            + stress[c, 2] * scaled[3 * d + 2]
                        )
            (dev0, div0), (dev1, div1) = kept
            bulk_sum = bulk_sum + div0 * div1
            for c in range(3):
                for m in range(c, 3):
                    product = dev0[c, m] * dev1[c, m]
                    shear_sum = shear_sum + (product if c == m else 2.0 * product)
        terms_ref[0, pl.ds(base, 8), :] += 2.0 * shear * shear_sum
        terms_ref[1, pl.ds(base, 8), :] += bulk * bulk_sum
        return carry

    lax.fori_loop(0, 16, elements, 0)
    nodal_force_ref[...] = jnp.dot(
        backward_ref[...], traction_ref[...], precision=highest, preferred_element_type=f32
    )
    sum_ref[...] = jnp.zeros_like(sum_ref)

    def scatter(g, carry):
        base = pl.multiple_of(g * 8, 8)
        row_ids = ids_ref[pl.ds(base, 8), :] >> 8
        values = nodal_force_ref[pl.ds(base, 8), :]
        high = values.astype(bf16).astype(f32)
        low = values - high
        pieces = []
        for r in range(8):
            mask = lax.broadcasted_iota(jnp.int32, (rows, 128), 0) == row_ids[r : r + 1, :]
            pieces.append(
                jnp.concatenate(
                    [
                        jnp.where(mask, part[r : r + 1, c * 128 : (c + 1) * 128], 0.0).astype(bf16)
                        for part in (high, low)
                        for c in range(12)
                    ],
                    axis=0,
                )
            )
        sum_ref[...] += lax.dot_general(
            jnp.concatenate(pieces, axis=1), onehot_ref[g], (((1,), (1,)), ((), ())),
            preferred_element_type=f32,
        )
        return carry

    lax.fori_loop(0, 16, scatter, 0)
    half = sum_ref.shape[0] // 2
    force_ref[...] = sum_ref[:half, :] + sum_ref[half:, :]

    border = jnp.concatenate([force_ref[c * rows : c * rows + 8, :] for c in range(12)], axis=0)
    upper, lower = split(border)
    onehot = slot_onehot(slots_ref)
    result = jnp.dot(
        jnp.concatenate([upper, lower], axis=1),
        jnp.concatenate([onehot, onehot], axis=0),
        preferred_element_type=f32,
    )
    outgoing = []
    for r in range(12):
        picked = pick_rows(result[:, r * 128 : (r + 1) * 128], slots_ref[r : r + 1, :] >> 8, 8)
        outgoing.append(jnp.concatenate(picked, axis=0))
    for p in range(sending_ref.shape[0]):
        block = jnp.zeros((12, WIDE), f32)
        for k in range(6):
            block = jnp.where(
                peers_ref[0, k] == p,
                jnp.concatenate([outgoing[2 * k], outgoing[2 * k + 1]], axis=1),
                block,
            )
        sending_ref[p] = block


def first_step(present_ref, *refs):
    refs[11][...] = jnp.zeros_like(refs[11])
    forces(present_ref, *refs)


def next_step(
    present_ref, earlier_ref, old_force_ref, arrived_ref, mass_ref, old_terms_ref,
    ids_ref, jacobian_ref, det_ref, moduli_ref, slots_ref, peers_ref,
    forward_ref, backward_ref, volume_ref,
    following_ref, force_ref, sending_ref, terms_ref, *scratch
):
    combine(present_ref, earlier_ref, old_force_ref, arrived_ref, mass_ref, slots_ref, peers_ref, following_ref)
    terms_ref[...] = old_terms_ref[...]
    forces(
        following_ref, ids_ref, jacobian_ref, det_ref, moduli_ref, slots_ref, peers_ref,
        forward_ref, backward_ref, volume_ref, force_ref, sending_ref, terms_ref, *scratch
    )


def per_device(
    wavefields,
    element_nodes,
    inverse_jacobian,
    jacobian_det,
    moduli,
    inverse_mass,
    neighbours,
    shared_counts,
    shared_points,
):
    events, _, point_count = wavefields.shape
    rows = point_count // WIDE
    domains = neighbours.shape[0]
    element_count = element_nodes.shape[1]
    parted = wavefields.reshape(events, 2, 2, 3 * rows, WIDE)
    present = parted[:, :, 0].reshape(12 * rows, WIDE)
    earlier = parted[:, :, 1].reshape(12 * rows, WIDE)
    mass = inverse_mass.reshape(rows, WIDE)
    ids = jnp.pad(element_nodes, ((0, 3), (0, 0)), constant_values=NOWHERE)
    own = lax.axis_index("dom")
    peers = lax.dynamic_slice_in_dim(neighbours, own, 1, 0)
    slot_count, capacity = shared_points.shape[1:]
    live = jnp.arange(capacity, dtype=jnp.int32)[None, :] < shared_counts[0][:, None]
    slots = jnp.where(live, shared_points[0], NOWHERE)
    slots = jnp.pad(slots, ((0, 0), (0, WIDE - capacity)), constant_values=NOWHERE)
    slots = slots.reshape(12, 128)
    moduli = jnp.pad(moduli, ((0, 0), (0, 3), (0, 0)))
    det = jacobian_det.reshape(1, element_count)
    forward, backward, volume = (jnp.asarray(table) for table in padded_tables())
    common = (ids, inverse_jacobian, det, moduli, slots, peers, forward, backward, volume)
    vmem = pl.BlockSpec(memory_space=pltpu.VMEM)
    smem = pl.BlockSpec(memory_space=pltpu.SMEM)
    common_specs = [vmem, vmem, vmem, vmem, vmem, smem, vmem, vmem, vmem]
    state = jax.ShapeDtypeStruct((12 * rows, WIDE), f32)
    made = (
        state,
        jax.ShapeDtypeStruct((domains, 12, WIDE), f32),
        jax.ShapeDtypeStruct((2, 128, 128), f32),
    )
    scratch = [
        pltpu.VMEM((16, WIDE, 1024), bf16),
        pltpu.VMEM((128, 12 * 128), f32),
        pltpu.VMEM((3 * 128, 12 * 128), f32),
        pltpu.VMEM((3 * 128, 12 * 128), f32),
        pltpu.VMEM((128, 12 * 128), f32),
        pltpu.VMEM((24 * rows, WIDE), f32),
    ]
    params = pltpu.CompilerParams(vmem_limit_bytes=50 * 1024 * 1024)

    def exchange(sending):
        return lax.all_to_all(sending, "dom", split_axis=0, concat_axis=0, tiled=True)

    force, sending, terms = pl.pallas_call(
        first_step,
        out_shape=made,
        in_specs=[vmem] + common_specs,
        out_specs=(vmem,) * 3,
        scratch_shapes=scratch,
        compiler_params=params,
    )(present, *common)
    for _ in range(STEPS - 1):
        arrived = exchange(sending)
        following, force, sending, terms = pl.pallas_call(
            next_step,
            out_shape=(state,) + made,
            in_specs=[vmem] * 6 + common_specs,
            out_specs=(vmem,) * 4,
            scratch_shapes=scratch,
            compiler_params=params,
        )(present, earlier, force, arrived, mass, terms, *common)
        earlier, present = present, following
    arrived = exchange(sending)
    following = pl.pallas_call(
        combine,
        out_shape=state,
        in_specs=[vmem] * 6 + [smem],
        out_specs=vmem,
        compiler_params=params,
    )(present, earlier, force, arrived, mass, slots, peers)
    earlier, present = present, following

    sharers = lax.axis_size("event")
    share_width = element_count // sharers
    spot = lax.axis_index("event")
    terms = terms[:, :125]
    if sharers == 2:
        low, high = terms[:, :, :share_width], terms[:, :, share_width:]
        theirs = lax.ppermute(jnp.where(spot == 0, high, low), "event", [(0, 1), (1, 0)])
        summed = jnp.where(spot == 0, low, high) + theirs
    else:
        summed = lax.dynamic_slice_in_dim(
            lax.psum(terms, "event"), spot * share_width, share_width, 2
        )
    sensitivity = kernel_weight * time_step * summed
    next_wavefields = jnp.stack(
        [present.reshape(events, 2, 3, point_count), earlier.reshape(events, 2, 3, point_count)],
        axis=2,
    ).reshape(events, 12, point_count)
    return (next_wavefields, sensitivity)


def solution(mesh):
    return jax.shard_map(
        per_device,
        mesh=mesh,
        in_specs=(
            P(("groups", "event"), None, "dom"),
            P(None, "dom"),
            P(None, "dom"),
            P("dom"),
            P(None, None, "dom"),
            P("dom"),
            P(),
            P("dom", None),
            P("dom", None, None),
        ),
        out_specs=(P(("groups", "event"), None, "dom"), P("groups", None, ("dom", "event"))),
        check_vma=False,
    )
```

profile of v0, /device:TPU:0, one launch (start us, length us, event | category | flops | bytes accessed | tf_op | source)
XLA Modules:
  0.0 89.7 jit_solution(12683474764532866448)
XLA Ops:
  0.6 0.0 copy-start
  0.6 0.0 copy-start.6
  0.7 0.8 bitcast_select_fusion
  1.5 0.8 pad.12.refs_0_.ids_ref
  2.3 0.0 copy-done.6
  2.3 1.6 %copy.20 = f32[2,12,8192]{2,1,0:T(8,128)S(1)} copy(f32[2,12,8192]{2,0,1:T(2,128)} %param.12) | data formatting | bytes 1572864 | tf_op args[0]
  3.9 0.2 reshape.20
  4.1 0.0 copy-start.2
  4.2 0.1 fusion
  4.2 0.0 copy-start.1
  4.2 0.0 copy-done
  4.3 0.0 copy-start.3
  4.3 0.0 copy-start.4
  4.3 0.0 copy-start.5
  4.3 0.8 copy-done.2
  5.1 0.1 copy-done.1
  5.2 0.0 copy-done.3
  5.2 0.0 copy-done.4
  5.2 0.0 copy-done.5
  5.2 27.4 %shard_map.131 = (f32[384,256]{1,0:T(8,128)S(1)}, f32[8,12,256]{2,1,0:T(8,128)}, f32[2,128,128]{2,1,0:T(8,128)S(1)}) custom-call(f32[384,256]{1,0:T(8,128)S(1)} %bitcast.7, s32[128,128]{1,0:T(8,128)S(1)} %pad.12.refs_0_.ids_ref, f32[9,128]{1,0:T(8,128)S(1)} %copy-done.4, f32[1,128]{1,0:T(1,128)S(1)} %bitcast.11, f32[2,128,128]{2,1,0:T(8,128)S(1)} %pad.13.refs_3_.moduli_ref, ...), custom_call_target="tpu_custom_call" | custom-call | tf_op jit(solution)/shard_map/pallas_call | solution.py:343
  32.6 0.0 copy-start.7
  32.6 7.4 %all-to-all-start = ((f32[8,12,256]{2,1,0:T(8,128)}), f32[8,12,256]{2,1,0:T(8,128)S(1)}, u32[]{:S(2)}, u32[]{:S(2)}) async-start(f32[8,12,256]{2,1,0:T(8,128)} %get-tuple-element.10), calls=%async_computation | async-start | bytes 262144 | tf_op jit(solution)/shard_map/all_to_all | solution.py:341
  40.0 0.0 copy-done.7
  40.0 7.3 %all-to-all-done.arrived_ref = f32[8,12,256]{2,1,0:T(8,128)S(1)} async-done(((f32[8,12,256]{2,1,0:T(8,128)}), f32[8,12,256]{2,1,0:T(8,128)S(1)}, u32[]{:S(2)}, u32[]{:S(2)}) %all-to-all-start) | async-done | bytes 98336 | tf_op jit(solution)/shard_map/all_to_all | solution.py:341
  47.3 27.9 %shard_map.132 = (f32[384,256]{1,0:T(8,128)S(1)}, f32[384,256]{1,0:T(8,128)S(1)}, f32[8,12,256]{2,1,0:T(8,128)}, f32[2,128,128]{2,1,0:T(8,128)S(1)}) custom-call(f32[384,256]{1,0:T(8,128)S(1)} %bitcast.8, f32[384,256]{1,0:T(8,128)S(1)} %bitcast.10, f32[384,256]{1,0:T(8,128)S(1)} %get-tuple-element.9.old_force_ref, ...), custom_call_target="tpu_custom_call" | custom-call | tf_op jit(solution)/shard_map/pallas_call | solution.py:353
  75.2 0.1 slice_select_fusion
  75.3 0.1 collective-permute-start
  75.4 3.4 %all-to-all-start.1 = ((f32[8,12,256]{2,1,0:T(8,128)}), f32[8,12,256]{2,1,0:T(8,128)S(1)}, u32[]{:S(2)}, u32[]{:S(2)}) async-start(f32[8,12,256]{2,1,0:T(8,128)} %get-tuple-element.14), calls=%async_computation.1 | async-start | bytes 262144 | tf_op jit(solution)/shard_map/all_to_all | solution.py:341
  78.8 0.2 stack_reshape.7
  79.0 0.0 collective-permute-done
  79.0 0.1 add_multiply_fusion
  79.2 0.7 copy.23
  79.9 6.8 %all-to-all-done.1.arrived_ref = f32[8,12,256]{2,1,0:T(8,128)S(1)} async-done(((f32[8,12,256]{2,1,0:T(8,128)}), f32[8,12,256]{2,1,0:T(8,128)S(1)}, u32[]{:S(2)}, u32[]{:S(2)}) %all-to-all-start.1) | async-done | bytes 98336 | tf_op jit(solution)/shard_map/all_to_all | solution.py:341
  86.7 1.1 %shard_map.133 = f32[384,256]{1,0:T(8,128)S(1)} custom-call(f32[384,256]{1,0:T(8,128)S(1)} %get-tuple-element.12.present_ref, f32[384,256]{1,0:T(8,128)S(1)} %bitcast.9, f32[384,256]{1,0:T(8,128)S(1)} %get-tuple-element.13.force_ref, f32[8,12,256]{2,1,0:T(8,128)S(1)} %all-to-all-done.1.arrived_ref, f32[32,256]{1,0:T(8,128)S(1)} %reshape.23.mass_ref, ...), custom_call_target="tpu_custom_call" | custom-call | tf_op jit(solution)/shard_map/pallas_call | solution.py:363
  87.7 0.2 stack_reshape.6
  88.0 0.3 pad_maximum_fusion
  88.2 1.5 %copy.22 = f32[2,2,2,3,8192]{4,0,3,2,1:T(2,128)} copy(f32[2,2,2,3,8192]{4,3,1,0,2:T(4,128)S(1)} %pad_maximum_fusion) | data formatting | bytes 1572864 | tf_op jit(solution)/shard_map/stack | solution.py:385
  (6 shorter events, 0.1 us)
Async XLA Ops:
  0.6 3.6 %copy-start = (s32[8,6]{1,0:T(8,128)S(1)}, s32[8,6]{1,0:T(8,128)}, u32[]{:S(2)}) copy-start(s32[8,6]{1,0:T(8,128)} %param.18) | copy-start | bytes 580
  0.6 1.7 %copy-start.6 = (f32[2,125,128]{2,0,1:T(2,128)S(1)}, f32[2,125,128]{2,0,1:T(2,128)}, u32[]{:S(2)}) copy-start(f32[2,125,128]{2,0,1:T(2,128)} %param.16) | copy-start | bytes 384004
  4.1 0.9 %copy-start.2 = (f32[384,128]{1,0:T(8,128)S(1)}, f32[384,128]{1,0:T(8,128)}, u32[]{:S(2)}) copy-start(f32[384,128]{1,0:T(8,128)} %constant.24.clone.refs_6_.forward_ref) | copy-start | bytes 589828
  4.2 1.0 %copy-start.1 = (f32[128,384]{1,0:T(8,128)S(1)}, f32[128,384]{1,0:T(8,128)}, u32[]{:S(2)}) copy-start(f32[128,384]{1,0:T(8,128)} %constant.25.clone.refs_7_.backward_ref) | copy-start | bytes 589828
  4.3 0.9 %copy-start.3 = (f32[128,128]{1,0:T(8,128)S(1)}, f32[128,128]{1,0:T(8,128)}, u32[]{:S(2)}) copy-start(f32[128,128]{1,0:T(8,128)} %constant.26.clone.refs_8_.volume_ref) | copy-start | bytes 196612
  4.3 0.9 %copy-start.4 = (f32[9,128]{1,0:T(8,128)S(1)}, f32[9,128]{1,0:T(8,128)}, u32[]{:S(2)}) copy-start(f32[9,128]{1,0:T(8,128)} %jacobian_ref.1) | copy-start | bytes 13828
  4.3 0.9 %copy-start.5 = (f32[128]{0:T(128)S(1)}, f32[128]{0:T(128)}, u32[]{:S(2)}) copy-start(f32[128]{0:T(128)} %param.15) | copy-start | bytes 1540
  32.6 7.4 %copy-start.7 = (f32[8192]{0:T(1024)S(1)}, f32[8192]{0:T(1024)}, u32[]{:S(2)}) copy-start(f32[8192]{0:T(1024)} %param.17) | copy-start | bytes 98308
  32.6 14.7 %all-to-all-start = ((f32[8,12,256]{2,1,0:T(8,128)}), f32[8,12,256]{2,1,0:T(8,128)S(1)}, u32[]{:S(2)}, u32[]{:S(2)}) async-start(f32[8,12,256]{2,1,0:T(8,128)} %get-tuple-element.10), calls=%async_computation | async-start | bytes 262144 | tf_op jit(solution)/shard_map/all_to_all | solution.py:341
  75.3 3.7 %collective-permute-start = (f32[2,125,64]{2,1,0:T(8,128)S(1)}, f32[2,125,64]{2,1,0:T(8,128)S(1)}, u32[]{:S(2)}, u32[]{:S(2)}) collective-permute-start(f32[2,125,64]{2,1,0:T(8,128)S(1)} %slice_select_fusion), channel_id=1, source_target_pairs={{0,1},{1,0},{2,3},{3,2},{4,5},{5,4},{6,7},{7,6},{8,9},{9,8},{10,11... | collective-permute-start | bytes 192008 | tf_op jit(solution)/shard_map/ppermute | solution.py:378
  75.4 11.2 %all-to-all-start.1 = ((f32[8,12,256]{2,1,0:T(8,128)}), f32[8,12,256]{2,1,0:T(8,128)S(1)}, u32[]{:S(2)}, u32[]{:S(2)}) async-start(f32[8,12,256]{2,1,0:T(8,128)} %get-tuple-element.14), calls=%async_computation.1 | async-start | bytes 262144 | tf_op jit(solution)/shard_map/all_to_all | solution.py:341
where the time goes:
time: 90.2 us; the launch traced here: 89.7 us
  Pallas kernels  56.4 us (63%)
  waiting for transfers between devices  14.1 us (16%)
  starting transfers between devices  10.8 us (12%)
  local copies, waits for them, and re-layouts  6.31 us (7%)
  other arithmetic  1.26 us (1%)
    pallas_call x1, Pallas kernels, per_device(): pl.pallas_call(next_step, out_shape=(state,) + made, in_specs=[vmem] * 6...  27.9 us
    pallas_call x1, Pallas kernels, per_device(): pl.pallas_call(first_step, out_shape=made, in_specs=[vmem] + common_specs...  27.4 us
    all_to_all x2, waiting for transfers between devices, exchange(): lax.all_to_all(sending, 'dom', split_axis=0, concat_axis=0, tiled=True)  14.1 us
    all_to_all x2, starting transfers between devices, exchange(): lax.all_to_all(sending, 'dom', split_axis=0, concat_axis=0, tiled=True)  10.8 us
    unnamed x19, local copies, waits for them, and re-layouts  3.25 us
    another operation x3, local copies, waits for them, and re-layouts, per_device(): jnp.stack([present.reshape(events, 2, 3, point_count), earlier.reshape(ev...  1.92 us
  transfers between devices with their start and end apart: 3, of which 2 were waited for; matrix products, arithmetic and copies ran while one was open for 1% of the time, Pallas kernels for 0%

commit v1 on v0

--- a/solution.py
+++ b/solution.py
@@ -57,8 +57,13 @@
 
 
 def columns_onehot(column_ids):
-    rows = lax.broadcasted_iota(jnp.int32, (WIDE, column_ids.shape[1]), 0)
-    return jnp.where(rows == column_ids, 1.0, 0.0).astype(bf16)
+    return onehot_rows(column_ids, WIDE)
+
+
+def onehot_rows(row_ids, count):
+    rows = lax.broadcasted_iota(jnp.int32, (count, 128), 0).astype(f32).astype(bf16)
+    wanted = jnp.broadcast_to(row_ids.astype(f32), (count, 128)).astype(bf16)
+    return jnp.where(rows == wanted, jnp.ones((), bf16), jnp.zeros((), bf16))
 
 
 def pick_rows(result, row_ids, group):
@@ -71,6 +76,32 @@
     ]
 
 
+def sum_sublanes(parts, sublane):
+    for width in (4, 2, 1):
+        first = (sublane & width) == 0
+        merged = []
+        for r in range(width):
+            near = jnp.where(first, parts[r], parts[r + width])
+            far = jnp.where(first, parts[r + width], parts[r])
+            if width == 4:
+                far = pltpu.roll(far, 4, 0)
+            else:
+                far = jnp.where(first, pltpu.roll(far, 8 - width, 0), pltpu.roll(far, width, 0))
+            merged.append(near + far)
+        parts = merged
+    return parts[0]
+
+
+def split_product(left, right):
+    left_upper, left_lower = split(left)
+    right_upper, right_lower = split(right)
+    return jnp.dot(
+        jnp.concatenate([left_upper, left_lower, left_upper], axis=1),
+        jnp.concatenate([right_upper, right_upper, right_lower], axis=0),
+        preferred_element_type=f32,
+    )
+
+
 def slot_onehot(slots_ref):
     return jnp.concatenate(
         [columns_onehot(slots_ref[r : r + 1, :] & (WIDE - 1)) for r in range(12)], axis=1
@@ -82,7 +113,7 @@
     rows = mass_ref.shape[0]
     blocks = []
     for k in range(6):
-        block = jnp.zeros((12, WIDE), f32)
+        block = jnp.zeros((16, WIDE), f32)
         for p in range(domains):
             block = jnp.where(peers_ref[0, k] == p, arrived_ref[p], block)
         blocks.append(block)
@@ -116,35 +147,34 @@
     present_ref, ids_ref, jacobian_ref, det_ref, moduli_ref, slots_ref, peers_ref,
     forward_ref, backward_ref, volume_ref,
     force_ref, sending_ref, terms_ref,
-    onehot_ref, nodal_ref, along_ref, traction_ref, nodal_force_ref, sum_ref,
+    nodal_ref, along_ref, traction_ref, nodal_force_ref, sum_ref,
 ):
     rows = present_ref.shape[0] // 12
-    upper, lower = split(present_ref[...])
-    table = jnp.concatenate([upper, lower], axis=1)
     sublane = lax.broadcasted_iota(jnp.int32, (8, 128), 0)
+    tiles = rows // 8
 
     def gather(g, carry):
         base = pl.multiple_of(g * 8, 8)
         ids = ids_ref[pl.ds(base, 8), :]
-        onehot = jnp.concatenate(
-            [columns_onehot((ids & (WIDE - 1))[r : r + 1, :]) for r in range(8)], axis=1
-        )
-        onehot_ref[g] = onehot
-        result = jnp.dot(
-            table, jnp.concatenate([onehot, onehot], axis=0), preferred_element_type=f32
-        )
-        row_ids = ids >> 8
-        gathered = [jnp.zeros((8, 128), f32)] * 12
+        lanes = [jnp.broadcast_to((ids & 127)[r : r + 1, :], (8, 128)) for r in range(8)]
+        keys = ids >> 7
+        masks = []
         for r in range(8):
-            picked = pick_rows(result[:, r * 128 : (r + 1) * 128], row_ids[r : r + 1, :], rows)
-            gathered = [jnp.where(sublane == r, picked[c], gathered[c]) for c in range(12)]
-        nodal_ref[pl.ds(base, 8), :] = jnp.concatenate(gathered, axis=1)
+            key = jnp.broadcast_to(keys[r : r + 1, :], (8, 128)) - 2 * sublane
+            masks.append([key == 16 * t + h for t in range(tiles) for h in range(2)])
+        for c in range(12):
+            found = [jnp.zeros((8, 128), f32)] * 8
+            for t in range(tiles):
+                for h in range(2):
+                    tile = present_ref[c * rows + t * 8 : c * rows + t * 8 + 8, h * 128 : h * 128 + 128]
+                    for r in range(8):
+                        taken = jnp.take_along_axis(tile, lanes[r], axis=1, mode="promise_in_bounds")
+                        found[r] = jnp.where(masks[r][2 * t + h], taken, found[r])
+            nodal_ref[pl.ds(base, 8), c * 128 : (c + 1) * 128] = sum_sublanes(found, sublane)
         return carry
 
     lax.fori_loop(0, 16, gather, 0)
-    along_ref[...] = jnp.dot(
-        forward_ref[...], nodal_ref[...], precision=highest, preferred_element_type=f32
-    )
+    along_ref[...] = split_product(forward_ref[...], nodal_ref[...])
 
     def elements(g, carry):
         base = pl.multiple_of(g * 8, 8)
@@ -211,9 +241,7 @@
         return carry
 
     lax.fori_loop(0, 16, elements, 0)
-    nodal_force_ref[...] = jnp.dot(
-        backward_ref[...], traction_ref[...], precision=highest, preferred_element_type=f32
-    )
+    nodal_force_ref[...] = split_product(backward_ref[...], traction_ref[...])
     sum_ref[...] = jnp.zeros_like(sum_ref)
 
     def scatter(g, carry):
@@ -223,21 +251,20 @@
         high = values.astype(bf16).astype(f32)
         low = values - high
         pieces = []
+        columns = []
         for r in range(8):
-            mask = lax.broadcasted_iota(jnp.int32, (rows, 128), 0) == row_ids[r : r + 1, :]
-            pieces.append(
-                jnp.concatenate(
-                    [
-                        jnp.where(mask, part[r : r + 1, c * 128 : (c + 1) * 128], 0.0).astype(bf16)
-                        for part in (high, low)
-                        for c in range(12)
-                    ],
-                    axis=0,
-                )
-            )
+            columns.append(columns_onehot((ids_ref[pl.ds(base, 8), :] & (WIDE - 1))[r : r + 1, :]))
+            chosen = onehot_rows(row_ids[r : r + 1, :], rows)
+            blocks = []
+            for part in (high, low):
+                for c in range(12):
+                    row = jnp.broadcast_to(part[r : r + 1, c * 128 : (c + 1) * 128], (16, 128))
+                    row = row.astype(bf16)
+                    blocks += [chosen[t : t + 16] * row for t in range(0, rows, 16)]
+            pieces.append(jnp.concatenate(blocks, axis=0))
         sum_ref[...] += lax.dot_general(
-            jnp.concatenate(pieces, axis=1), onehot_ref[g], (((1,), (1,)), ((), ())),
-            preferred_element_type=f32,
+            jnp.concatenate(pieces, axis=1), jnp.concatenate(columns, axis=1),
+            (((1,), (1,)), ((), ())), preferred_element_type=f32,
         )
         return carry
 
@@ -256,9 +283,9 @@
     outgoing = []
     for r in range(12):
         picked = pick_rows(result[:, r * 128 : (r + 1) * 128], slots_ref[r : r + 1, :] >> 8, 8)
-        outgoing.append(jnp.concatenate(picked, axis=0))
+        outgoing.append(jnp.concatenate(picked + [jnp.zeros((4, 128), f32)], axis=0))
     for p in range(sending_ref.shape[0]):
-        block = jnp.zeros((12, WIDE), f32)
+        block = jnp.zeros((16, WIDE), f32)
         for k in range(6):
             block = jnp.where(
                 peers_ref[0, k] == p,
@@ -266,6 +293,35 @@
                 block,
             )
         sending_ref[p] = block
+
+
+def swap_blocks(sending_ref, arrived_ref, send_sem, recv_sem):
+    domains = sending_ref.shape[0]
+    me = lax.axis_index("dom")
+    barrier = pltpu.get_barrier_semaphore()
+    for offset in range(1, domains):
+        pl.semaphore_signal(
+            barrier, inc=1, device_id={"dom": lax.rem(me + offset, domains)},
+            device_id_type=pl.DeviceIdType.MESH,
+        )
+    pl.semaphore_wait(barrier, domains - 1)
+    copies = []
+    for offset in range(1, domains):
+        target = lax.rem(me + offset, domains)
+        copies.append(
+            pltpu.make_async_remote_copy(
+                src_ref=sending_ref.at[target],
+                dst_ref=arrived_ref.at[me],
+                send_sem=send_sem.at[offset],
+                recv_sem=recv_sem.at[offset],
+                device_id={"dom": target},
+                device_id_type=pl.DeviceIdType.MESH,
+            )
+        )
+        copies[-1].start()
+    arrived_ref[me] = sending_ref[me]
+    for copy in copies:
+        copy.wait()
 
 
 def first_step(present_ref, *refs):
@@ -324,11 +380,10 @@
     state = jax.ShapeDtypeStruct((12 * rows, WIDE), f32)
     made = (
         state,
-        jax.ShapeDtypeStruct((domains, 12, WIDE), f32),
+        jax.ShapeDtypeStruct((domains, 16, WIDE), f32),
         jax.ShapeDtypeStruct((2, 128, 128), f32),
     )
     scratch = [
-        pltpu.VMEM((16, WIDE, 1024), bf16),
         pltpu.VMEM((128, 12 * 128), f32),
         pltpu.VMEM((3 * 128, 12 * 128), f32),
         pltpu.VMEM((3 * 128, 12 * 128), f32),
@@ -338,7 +393,17 @@
     params = pltpu.CompilerParams(vmem_limit_bytes=50 * 1024 * 1024)
 
     def exchange(sending):
-        return lax.all_to_all(sending, "dom", split_axis=0, concat_axis=0, tiled=True)
+        return pl.pallas_call(
+            swap_blocks,
+            out_shape=jax.ShapeDtypeStruct(sending.shape, sending.dtype),
+            in_specs=[vmem],
+            out_specs=vmem,
+            scratch_shapes=[
+                pltpu.SemaphoreType.DMA((domains,)),
+                pltpu.SemaphoreType.DMA((domains,)),
+            ],
+            compiler_params=pltpu.CompilerParams(collective_id=0, has_side_effects=True),
+        )(sending)
 
     force, sending, terms = pl.pallas_call(
         first_step,

time: 90.2 us -> 133 us (1.47)
  Pallas kernels: 56.4 us -> 121 us
  waiting for transfers between devices: 14.1 us -> 0.01 us
  starting transfers between devices: 10.8 us -> 0.01 us
  local copies, waits for them, and re-layouts: 6.31 us -> 8.9 us
    pallas_call x1, Pallas kernels: 27.9 us -> 50.4 us  [per_device(): pl.pallas_call(next_step, out_shape=(state,) + made, in_specs=[vmem] * 6...]
    pallas_call x1, Pallas kernels: 27.4 us -> 49.5 us  [per_device(): pl.pallas_call(first_step, out_shape=made, in_specs=[vmem] + common_specs...]
    pallas_call x0 -> x2, Pallas kernels: none -> 20.4 us  [exchange(): pl.pallas_call(swap_blocks, out_shape=jax.ShapeDtypeStruct(sending.shape,...]
    all_to_all x2 -> x0, waiting for transfers between devices: 14.1 us -> none  [exchange(): lax.all_to_all(sending, 'dom', split_axis=0, concat_axis=0, tiled=True)]
    all_to_all x2 -> x0, starting transfers between devices: 10.8 us -> none  [exchange(): lax.all_to_all(sending, 'dom', split_axis=0, concat_axis=0, tiled=True)]
    unnamed x19 -> x31, local copies, waits for them, and re-layouts: 3.25 us -> 6.67 us
  transfers between devices with their start and end apart: 3 -> 1, of which waited for: 2 -> 0; matrix products, arithmetic and copies ran while one was open for 1% -> 2% of each run, Pallas kernels for 0% -> 8%
where the time goes in v1:
time: 133 us; the launch traced here: 132 us
  Pallas kernels  121 us (91%)
  local copies, waits for them, and re-layouts  8.9 us (7%)
    pallas_call x1, Pallas kernels, per_device(): pl.pallas_call(next_step, out_shape=(state,) + made, in_specs=[vmem] * 6...  50.4 us
    pallas_call x1, Pallas kernels, per_device(): pl.pallas_call(first_step, out_shape=made, in_specs=[vmem] + common_specs...  49.5 us
    pallas_call x2, Pallas kernels, exchange(): pl.pallas_call(swap_blocks, out_shape=jax.ShapeDtypeStruct(sending.shape,...  20.4 us
    unnamed x31, local copies, waits for them, and re-layouts  6.67 us
  transfers between devices with their start and end apart: 1, of which 0 were waited for; matrix products, arithmetic and copies ran while one was open for 2% of the time, Pallas kernels for 8%

profile of v1, /device:TPU:0, one launch (start us, length us, event | category | flops | bytes accessed | tf_op | source)
XLA Modules:
  0.0 132.4 jit_solution(17232975098444366122)
XLA Ops:
  0.6 0.0 copy-start
  0.6 0.0 copy-start.13
  0.7 0.0 copy-start.12
  0.7 0.0 copy-start.11
  0.7 0.0 copy-start.10
  0.7 0.7 copy-done.13
  1.3 0.7 bitcast_select_fusion
  2.1 0.0 copy-done.12
  2.1 0.0 copy-done.11
  2.1 0.0 copy-done.10
  2.2 1.6 %copy.20 = f32[2,12,8192]{2,1,0:T(8,128)S(1)} copy(f32[2,12,8192]{2,0,1:T(2,128)} %param.12) | data formatting | bytes 1572864 | tf_op args[0]
  3.8 0.2 reshape.20
  4.0 0.0 copy-start.2
  4.0 0.1 fusion
  4.0 0.0 copy-start.1
  4.1 0.0 copy-done
  4.1 0.0 copy-start.5
  4.1 0.0 copy-start.8
  4.1 0.0 copy-start.9
  4.1 0.8 copy-done.2
  4.9 0.1 copy-done.1
  5.0 0.0 copy-done.5
  5.0 0.0 copy-done.8
  5.0 0.0 copy-done.9
  5.0 49.5 %shard_map.131 = (f32[384,256]{1,0:T(8,128)S(1)}, f32[8,16,256]{2,1,0:T(8,128)S(1)}, f32[2,128,128]{2,1,0:T(8,128)S(1)}) custom-call(f32[384,256]{1,0:T(8,128)S(1)} %bitcast.7, s32[128,128]{1,0:T(8,128)S(1)} %pad.12.refs_0_.ids_ref, f32[9,128]{1,0:T(8,128)S(1)} %copy-done.8, f32[1,128]{1,0:T(1,128)S(1)} %bitcast.11, ...), custom_call_target="tpu_custom_call" | custom-call | tf_op jit(solution)/shard_map/pallas_call | solution.py:408
  54.5 0.0 copy-start.7
  54.5 0.6 copy-done.7
  55.2 10.8 %shard_map.132.arrived_ref = f32[8,16,256]{2,1,0:T(8,128)} custom-call(f32[8,16,256]{2,1,0:T(8,128)} %copy-done.7), custom_call_target="tpu_custom_call" | custom-call | tf_op jit(solution)/shard_map/pallas_call | solution.py:396
  66.0 0.0 copy-start.4
  66.1 0.9 copy-done.4
  67.0 50.4 %shard_map.133 = (f32[384,256]{1,0:T(8,128)S(1)}, f32[384,256]{1,0:T(8,128)S(1)}, f32[8,16,256]{2,1,0:T(8,128)S(1)}, f32[2,128,128]{2,1,0:T(8,128)S(1)}) custom-call(f32[384,256]{1,0:T(8,128)S(1)} %bitcast.8, f32[384,256]{1,0:T(8,128)S(1)} %bitcast.10, f32[384,256]{1,0:T(8,128)S(1)} %get-tuple-element.9.old_force_ref, f32[8,16,256]{2,1,0:T(8,128)S(1)} %copy-done.4, ...), custom_call_target="tpu_custom_call" | custom-call | tf_op jit(solution)/shard_map/pallas_call | solution.py:418
  117.4 0.0 copy-start.6
  117.4 0.1 slice_select_fusion
  117.5 0.5 copy-done.6
  118.0 0.0 collective-permute-start
  118.0 9.6 %shard_map.134.arrived_ref = f32[8,16,256]{2,1,0:T(8,128)} custom-call(f32[8,16,256]{2,1,0:T(8,128)} %copy-done.6), custom_call_target="tpu_custom_call" | custom-call | tf_op jit(solution)/shard_map/pallas_call | solution.py:396
  127.6 0.0 copy-start.3
  127.7 0.2 stack_reshape.7
  127.9 0.7 copy-done.3
  128.5 1.0 shard_map.135
  129.5 0.2 stack_reshape.6
  129.8 0.3 pad_maximum_fusion
  130.0 1.5 %copy.22 = f32[2,2,2,3,8192]{4,0,3,2,1:T(2,128)} copy(f32[2,2,2,3,8192]{4,3,1,0,2:T(4,128)S(1)} %pad_maximum_fusion) | data formatting | bytes 1572864 | tf_op jit(solution)/shard_map/stack | solution.py:450
  131.5 0.0 collective-permute-done
  131.5 0.1 add_multiply_fusion
  131.6 0.7 copy.23
  (7 shorter events, 0.1 us)
Async XLA Ops:
  0.6 3.4 %copy-start = (s32[8,6]{1,0:T(8,128)S(1)}, s32[8,6]{1,0:T(8,128)}, u32[]{:S(2)}) copy-start(s32[8,6]{1,0:T(8,128)} %param.18) | copy-start | bytes 580
  0.6 0.7 copy-start.13
  0.7 1.4 %copy-start.12 = (f32[8192]{0:T(1024)S(1)}, f32[8192]{0:T(1024)}, u32[]{:S(2)}) copy-start(f32[8192]{0:T(1024)} %param.17) | copy-start | bytes 98308
  0.7 1.4 %copy-start.11 = (s32[125,128]{1,0:T(8,128)S(1)}, s32[125,128]{1,0:T(8,128)}, u32[]{:S(2)}) copy-start(s32[125,128]{1,0:T(8,128)} %param.13) | copy-start | bytes 192004
  0.7 1.5 %copy-start.10 = (f32[2,125,128]{2,0,1:T(2,128)S(1)}, f32[2,125,128]{2,0,1:T(2,128)}, u32[]{:S(2)}) copy-start(f32[2,125,128]{2,0,1:T(2,128)} %param.16) | copy-start | bytes 384004
  4.0 0.9 copy-start.2
  4.0 1.0 copy-start.1
  4.1 0.9 copy-start.5
  4.1 0.9 copy-start.8
  4.1 0.9 copy-start.9
  54.5 0.7 copy-start.7
  66.0 0.9 copy-start.4
  117.4 0.7 copy-start.6
  118.0 13.5 %collective-permute-start = (f32[2,125,64]{2,1,0:T(8,128)S(1)}, f32[2,125,64]{2,1,0:T(8,128)S(1)}, u32[]{:S(2)}, u32[]{:S(2)}) collective-permute-start(f32[2,125,64]{2,1,0:T(8,128)S(1)} %slice_select_fusion), channel_id=1, source_target_pairs={{0,1},{1,0},{2,3},{3,2},{4,5},{5,4},{6,7},{7,6},{8,9},{9,8},{10,11... | collective-permute-start | bytes 192008 | tf_op jit(solution)/shard_map/ppermute | solution.py:443
  127.6 0.9 copy-start.3

commit v2 on v1

--- a/solution.py
+++ b/solution.py
@@ -143,33 +143,65 @@
         following_ref[where, :] = 2.0 * present_ref[where, :] - earlier_ref[where, :] - mass * total
 
 
+def add_rows(g, values_ref, ids_ref, sum_ref, rows):
+    base = pl.multiple_of(g * 8, 8)
+    ids = ids_ref[pl.ds(base, 8), :]
+    row_ids = ids >> 8
+    column_ids = ids & (WIDE - 1)
+    values = values_ref[pl.ds(base, 8), :]
+    high = values.astype(bf16).astype(f32)
+    low = values - high
+    pieces = []
+    columns = []
+    for r in range(8):
+        columns.append(columns_onehot(column_ids[r : r + 1, :]))
+        chosen = onehot_rows(row_ids[r : r + 1, :], rows)
+        blocks = []
+        for part in (high, low):
+            for c in range(12):
+                row = jnp.broadcast_to(part[r : r + 1, c * 128 : (c + 1) * 128], (16, 128))
+                row = row.astype(bf16)
+                blocks += [chosen[t : t + 16] * row for t in range(0, rows, 16)]
+        pieces.append(jnp.concatenate(blocks, axis=0))
+    sum_ref[...] += lax.dot_general(
+        jnp.concatenate(pieces, axis=1), jnp.concatenate(columns, axis=1),
+        (((1,), (1,)), ((), ())), preferred_element_type=f32,
+    )
+
+
 def forces(
-    present_ref, ids_ref, jacobian_ref, det_ref, moduli_ref, slots_ref, peers_ref,
+    present_ref, ids_ref, border_ids_ref, jacobian_ref, det_ref, moduli_ref, slots_ref, peers_ref,
     forward_ref, backward_ref, volume_ref,
-    force_ref, sending_ref, terms_ref,
-    nodal_ref, along_ref, traction_ref, nodal_force_ref, sum_ref,
+    nodal_force_ref, sending_ref, terms_ref,
+    nodal_ref, along_ref, traction_ref, packed_ref, sum_ref,
 ):
     rows = present_ref.shape[0] // 12
     sublane = lax.broadcasted_iota(jnp.int32, (8, 128), 0)
     tiles = rows // 8
+    upper, lower = split(present_ref[...])
+    table = jnp.concatenate([upper, lower], axis=1)
 
     def gather(g, carry):
         base = pl.multiple_of(g * 8, 8)
         ids = ids_ref[pl.ds(base, 8), :]
-        lanes = [jnp.broadcast_to((ids & 127)[r : r + 1, :], (8, 128)) for r in range(8)]
-        keys = ids >> 7
+        onehot = jnp.concatenate(
+            [columns_onehot((ids & (WIDE - 1))[r : r + 1, :]) for r in range(8)], axis=1
+        )
+        result = jnp.dot(
+            table, jnp.concatenate([onehot, onehot], axis=0), preferred_element_type=f32
+        )
+        row_ids = ids >> 8
         masks = []
         for r in range(8):
-            key = jnp.broadcast_to(keys[r : r + 1, :], (8, 128)) - 2 * sublane
-            masks.append([key == 16 * t + h for t in range(tiles) for h in range(2)])
+            key = jnp.broadcast_to(row_ids[r : r + 1, :], (8, 128)) - sublane
+            masks.append([key == 8 * t for t in range(tiles)])
         for c in range(12):
             found = [jnp.zeros((8, 128), f32)] * 8
-            for t in range(tiles):
-                for h in range(2):
-                    tile = present_ref[c * rows + t * 8 : c * rows + t * 8 + 8, h * 128 : h * 128 + 128]
-                    for r in range(8):
-                        taken = jnp.take_along_axis(tile, lanes[r], axis=1, mode="promise_in_bounds")
-                        found[r] = jnp.where(masks[r][2 * t + h], taken, found[r])
+            for r in range(8):
+                for t in range(tiles):
+                    first = c * rows + t * 8
+                    tile = result[first : first + 8, r * 128 : (r + 1) * 128]
+                    found[r] = jnp.where(masks[r][t], tile, found[r])
             nodal_ref[pl.ds(base, 8), c * 128 : (c + 1) * 128] = sum_sublanes(found, sublane)
         return carry
 
@@ -242,37 +274,23 @@
 
     lax.fori_loop(0, 16, elements, 0)
     nodal_force_ref[...] = split_product(backward_ref[...], traction_ref[...])
+    lane = lax.broadcasted_iota(jnp.int32, (32, 128), 1)
+    for c in range(12):
+        column = slice(c * 128, (c + 1) * 128)
+        packed = nodal_force_ref[:32, column]
+        for b in range(1, 4):
+            moved = pltpu.roll(nodal_force_ref[b * 32 : (b + 1) * 32, column], 32 * b, 1)
+            packed = jnp.where(lane >= 32 * b, moved, packed)
+        packed_ref[:, column] = packed
     sum_ref[...] = jnp.zeros_like(sum_ref)
 
-    def scatter(g, carry):
-        base = pl.multiple_of(g * 8, 8)
-        row_ids = ids_ref[pl.ds(base, 8), :] >> 8
-        values = nodal_force_ref[pl.ds(base, 8), :]
-        high = values.astype(bf16).astype(f32)
-        low = values - high
-        pieces = []
-        columns = []
-        for r in range(8):
-            columns.append(columns_onehot((ids_ref[pl.ds(base, 8), :] & (WIDE - 1))[r : r + 1, :]))
-            chosen = onehot_rows(row_ids[r : r + 1, :], rows)
-            blocks = []
-            for part in (high, low):
-                for c in range(12):
-                    row = jnp.broadcast_to(part[r : r + 1, c * 128 : (c + 1) * 128], (16, 128))
-                    row = row.astype(bf16)
-                    blocks += [chosen[t : t + 16] * row for t in range(0, rows, 16)]
-            pieces.append(jnp.concatenate(blocks, axis=0))
-        sum_ref[...] += lax.dot_general(
-            jnp.concatenate(pieces, axis=1), jnp.concatenate(columns, axis=1),
-            (((1,), (1,)), ((), ())), preferred_element_type=f32,
-        )
+    def border_rows(g, carry):
+        add_rows(g, packed_ref, border_ids_ref, sum_ref, 16)
         return carry
 
-    lax.fori_loop(0, 16, scatter, 0)
-    half = sum_ref.shape[0] // 2
-    force_ref[...] = sum_ref[:half, :] + sum_ref[half:, :]
-
-    border = jnp.concatenate([force_ref[c * rows : c * rows + 8, :] for c in range(12)], axis=0)
+    lax.fori_loop(0, 4, border_rows, 0)
+    sums = sum_ref[:192, :] + sum_ref[192:, :]
+    border = jnp.concatenate([sums[c * 16 : c * 16 + 8, :] for c in range(12)], axis=0)
     upper, lower = split(border)
     onehot = slot_onehot(slots_ref)
     result = jnp.dot(
@@ -295,7 +313,9 @@
         sending_ref[p] = block
 
 
-def swap_blocks(sending_ref, arrived_ref, send_sem, recv_sem):
+def swap_and_sum(
+    sending_ref, nodal_force_ref, ids_ref, force_ref, arrived_ref, sum_ref, send_sem, recv_sem
+):
     domains = sending_ref.shape[0]
     me = lax.axis_index("dom")
     barrier = pltpu.get_barrier_semaphore()
@@ -320,26 +340,35 @@
         )
         copies[-1].start()
     arrived_ref[me] = sending_ref[me]
+    sum_ref[...] = jnp.zeros_like(sum_ref)
+    half = sum_ref.shape[0] // 2
+
+    def node_rows(g, carry):
+        add_rows(g, nodal_force_ref, ids_ref, sum_ref, half // 12)
+        return carry
+
+    lax.fori_loop(0, 16, node_rows, 0)
+    force_ref[...] = sum_ref[:half, :] + sum_ref[half:, :]
     for copy in copies:
         copy.wait()
 
 
 def first_step(present_ref, *refs):
-    refs[11][...] = jnp.zeros_like(refs[11])
+    refs[12][...] = jnp.zeros_like(refs[12])
     forces(present_ref, *refs)
 
 
 def next_step(
     present_ref, earlier_ref, old_force_ref, arrived_ref, mass_ref, old_terms_ref,
-    ids_ref, jacobian_ref, det_ref, moduli_ref, slots_ref, peers_ref,
+    ids_ref, border_ids_ref, jacobian_ref, det_ref, moduli_ref, slots_ref, peers_ref,
     forward_ref, backward_ref, volume_ref,
-    following_ref, force_ref, sending_ref, terms_ref, *scratch
+    following_ref, nodal_force_ref, sending_ref, terms_ref, *scratch
 ):
     combine(present_ref, earlier_ref, old_force_ref, arrived_ref, mass_ref, slots_ref, peers_ref, following_ref)
     terms_ref[...] = old_terms_ref[...]
     forces(
-        following_ref, ids_ref, jacobian_ref, det_ref, moduli_ref, slots_ref, peers_ref,
-        forward_ref, backward_ref, volume_ref, force_ref, sending_ref, terms_ref, *scratch
+        following_ref, ids_ref, border_ids_ref, jacobian_ref, det_ref, moduli_ref, slots_ref, peers_ref,
+        forward_ref, backward_ref, volume_ref, nodal_force_ref, sending_ref, terms_ref, *scratch
     )
 
 
@@ -373,13 +402,14 @@
     moduli = jnp.pad(moduli, ((0, 0), (0, 3), (0, 0)))
     det = jacobian_det.reshape(1, element_count)
     forward, backward, volume = (jnp.asarray(table) for table in padded_tables())
-    common = (ids, inverse_jacobian, det, moduli, slots, peers, forward, backward, volume)
+    border_ids = jnp.concatenate([ids[b * 32 : (b + 1) * 32, :32] for b in range(4)], axis=1)
+    common = (ids, border_ids, inverse_jacobian, det, moduli, slots, peers, forward, backward, volume)
     vmem = pl.BlockSpec(memory_space=pltpu.VMEM)
     smem = pl.BlockSpec(memory_space=pltpu.SMEM)
-    common_specs = [vmem, vmem, vmem, vmem, vmem, smem, vmem, vmem, vmem]
+    common_specs = [vmem, vmem, vmem, vmem, vmem, vmem, smem, vmem, vmem, vmem]
     state = jax.ShapeDtypeStruct((12 * rows, WIDE), f32)
     made = (
-        state,
+        jax.ShapeDtypeStruct((128, 12 * 128), f32),
         jax.ShapeDtypeStruct((domains, 16, WIDE), f32),
         jax.ShapeDtypeStruct((2, 128, 128), f32),
     )
@@ -387,25 +417,28 @@
         pltpu.VMEM((128, 12 * 128), f32),
         pltpu.VMEM((3 * 128, 12 * 128), f32),
         pltpu.VMEM((3 * 128, 12 * 128), f32),
-        pltpu.VMEM((128, 12 * 128), f32),
-        pltpu.VMEM((24 * rows, WIDE), f32),
+        pltpu.VMEM((32, 12 * 128), f32),
+        pltpu.VMEM((24 * 16, WIDE), f32),
     ]
     params = pltpu.CompilerParams(vmem_limit_bytes=50 * 1024 * 1024)
 
-    def exchange(sending):
+    def exchange(sending, nodal_force):
         return pl.pallas_call(
-            swap_blocks,
-            out_shape=jax.ShapeDtypeStruct(sending.shape, sending.dtype),
-            in_specs=[vmem],
-            out_specs=vmem,
+            swap_and_sum,
+            out_shape=(state, jax.ShapeDtypeStruct(sending.shape, sending.dtype)),
+            in_specs=[vmem] * 3,
+            out_specs=(vmem, vmem),
             scratch_shapes=[
+                pltpu.VMEM((24 * rows, WIDE), f32),
                 pltpu.SemaphoreType.DMA((domains,)),
                 pltpu.SemaphoreType.DMA((domains,)),
             ],
-            compiler_params=pltpu.CompilerParams(collective_id=0, has_side_effects=True),
-        )(sending)
-
-    force, sending, terms = pl.pallas_call(
+            compiler_params=pltpu.CompilerParams(
+                collective_id=0, has_side_effects=True, vmem_limit_bytes=50 * 1024 * 1024
+            ),
+        )(sending, nodal_force, ids)
+
+    nodal_force, sending, terms = pl.pallas_call(
         first_step,
         out_shape=made,
         in_specs=[vmem] + common_specs,
@@ -414,8 +447,8 @@
         compiler_params=params,
     )(present, *common)
     for _ in range(STEPS - 1):
-        arrived = exchange(sending)
-        following, force, sending, terms = pl.pallas_call(
+        force, arrived = exchange(sending, nodal_force)
+        following, nodal_force, sending, terms = pl.pallas_call(
             next_step,
             out_shape=(state,) + made,
             in_specs=[vmem] * 6 + common_specs,
@@ -424,7 +457,7 @@
             compiler_params=params,
         )(present, earlier, force, arrived, mass, terms, *common)
         earlier, present = present, following
-    arrived = exchange(sending)
+    force, arrived = exchange(sending, nodal_force)
     following = pl.pallas_call(
         combine,
         out_shape=state,

time: 133 us -> 67.7 us (0.51)
  Pallas kernels: 121 us -> 58.9 us
  local copies, waits for them, and re-layouts: 8.9 us -> 7 us
    pallas_call x1, Pallas kernels: 50.4 us -> 15.5 us  [per_device(): pl.pallas_call(next_step, out_shape=(state,) + made, in_specs=[vmem] * 6...]
    pallas_call x1, Pallas kernels: 49.5 us -> 15.1 us  [per_device(): pl.pallas_call(first_step, out_shape=made, in_specs=[vmem] + common_specs...]
    pallas_call x2, Pallas kernels: 20.4 us -> 27.3 us  [exchange(): pl.pallas_call(swap_and_sum, out_shape=(state, jax.ShapeDtypeStruct(sendi...]
    unnamed x31 -> x25, local copies, waits for them, and re-layouts: 6.67 us -> 3.95 us
  transfers between devices with their start and end apart: 1 -> 1, of which waited for: 0 -> 0; matrix products, arithmetic and copies ran while one was open for 2% -> 3% of each run, Pallas kernels for 8% -> 18%
where the time goes in v2:
time: 67.7 us; the launch traced here: 67.4 us
  Pallas kernels  58.9 us (87%)
  local copies, waits for them, and re-layouts  7 us (10%)
  between operations  0.87 us (1%)
    pallas_call x2, Pallas kernels, exchange(): pl.pallas_call(swap_and_sum, out_shape=(state, jax.ShapeDtypeStruct(sendi...  27.3 us
    pallas_call x1, Pallas kernels, per_device(): pl.pallas_call(next_step, out_shape=(state,) + made, in_specs=[vmem] * 6...  15.5 us
    pallas_call x1, Pallas kernels, per_device(): pl.pallas_call(first_step, out_shape=made, in_specs=[vmem] + common_specs...  15.1 us
    unnamed x25, local copies, waits for them, and re-layouts  3.95 us
    another operation x3, local copies, waits for them, and re-layouts, per_device(): jnp.stack([present.reshape(events, 2, 3, point_count), earlier.reshape(ev...  1.92 us
  transfers between devices with their start and end apart: 1, of which 0 were waited for; matrix products, arithmetic and copies ran while one was open for 3% of the time, Pallas kernels for 18%

profile of v2, /device:TPU:0, one launch (start us, length us, event | category | flops | bytes accessed | tf_op | source)
XLA Modules:
  0.0 67.4 jit_solution(4182170832459406621)
XLA Ops:
  0.6 0.0 copy-start
  0.7 0.0 copy-start.6
  0.7 0.0 copy-start.9
  0.7 0.8 %fusion.1 = (s32[32,32]{1,0:T(8,128)S(1)}, s32[32,32]{1,0:T(8,128)S(1)}, s32[32,32]{1,0:T(8,128)S(1)}, s32[32,32]{1,0:T(8,128)S(1)}) fusion(s32[125,128]{1,0:T(8,128)} %param.13), kind=kLoop, calls=%fused_computation.9 | loop fusion | bytes 131072 | tf_op jit(solution)/shard_map/slice | solution.py:405
  1.5 0.0 copy-done.6
  1.5 0.0 copy-start.10
  1.5 0.0 copy-start.7
  1.5 0.0 copy-start.8
  1.5 0.0 copy-done.9
  1.5 0.6 copy-done.10
  2.1 0.1 bitcast_select_fusion
  2.2 0.1 copy-done.8
  2.3 0.1 copy-done.7
  2.4 1.6 %copy.20 = f32[2,12,8192]{2,1,0:T(8,128)S(1)} copy(f32[2,12,8192]{2,0,1:T(2,128)} %param.12) | data formatting | bytes 1572864 | tf_op args[0]
  4.0 0.2 reshape.20
  4.2 0.0 copy-start.2
  4.2 0.1 fusion
  4.3 0.0 copy-start.1
  4.3 0.0 copy-done
  4.4 0.0 copy-start.3
  4.4 0.0 copy-start.4
  4.4 0.1 pad_add_fusion.refs_1_.border_ids_ref
  4.5 0.0 copy-start.5
  4.5 0.7 copy-done.2
  5.2 0.1 copy-done.1
  5.3 0.0 copy-done.3
  5.3 0.0 copy-done.4
  5.3 0.0 copy-done.5
  5.3 15.1 %shard_map.131 = (f32[128,1536]{1,0:T(8,128)S(1)}, f32[8,16,256]{2,1,0:T(8,128)S(1)}, f32[2,128,128]{2,1,0:T(8,128)S(1)}) custom-call(f32[384,256]{1,0:T(8,128)S(1)} %bitcast.7, s32[128,128]{1,0:T(8,128)S(1)} %pad.12.refs_0_.ids_ref, s32[32,128]{1,0:T(8,128)S(1)} %pad_add_fusion.refs_1_.border_ids_ref, f32[9,128]{1,0:T(8,128)S(1)} %copy-done.4, ...), custom_call_target="tpu_custom_call" | custom-call | tf_op jit(solution)/shard_map/pallas_call | solution.py:441
  20.4 16.3 %shard_map.132 = (f32[384,256]{1,0:T(8,128)S(1)}, f32[8,16,256]{2,1,0:T(8,128)S(1)}) custom-call(f32[8,16,256]{2,1,0:T(8,128)S(1)} %get-tuple-element.13.sending_ref, f32[128,1536]{1,0:T(8,128)S(1)} %get-tuple-element.14.nodal_force_ref, s32[128,128]{1,0:T(8,128)S(1)} %pad.12.refs_0_.ids_ref), custom_call_target="tpu_custom_call" | custom-call | tf_op jit(solution)/shard_map/pallas_call | solution.py:426
  36.7 15.5 %shard_map.133 = (f32[384,256]{1,0:T(8,128)S(1)}, f32[128,1536]{1,0:T(8,128)S(1)}, f32[8,16,256]{2,1,0:T(8,128)S(1)}, f32[2,128,128]{2,1,0:T(8,128)S(1)}) custom-call(f32[384,256]{1,0:T(8,128)S(1)} %bitcast.8, f32[384,256]{1,0:T(8,128)S(1)} %bitcast.10, f32[384,256]{1,0:T(8,128)S(1)} %get-tuple-element.15.old_force_ref, ...), custom_call_target="tpu_custom_call" | custom-call | tf_op jit(solution)/shard_map/pallas_call | solution.py:451
  52.2 0.1 slice_select_fusion
  52.3 0.1 collective-permute-start
  52.4 0.2 stack_reshape.7
  52.6 11.0 %shard_map.134 = (f32[384,256]{1,0:T(8,128)S(1)}, f32[8,16,256]{2,1,0:T(8,128)S(1)}) custom-call(f32[8,16,256]{2,1,0:T(8,128)S(1)} %get-tuple-element.19.sending_ref, f32[128,1536]{1,0:T(8,128)S(1)} %get-tuple-element.20.nodal_force_ref, s32[128,128]{1,0:T(8,128)S(1)} %pad.12.refs_0_.ids_ref), custom_call_target="tpu_custom_call" | custom-call | tf_op jit(solution)/shard_map/pallas_call | solution.py:426
  63.6 1.0 %shard_map.135 = f32[384,256]{1,0:T(8,128)S(1)} custom-call(f32[384,256]{1,0:T(8,128)S(1)} %get-tuple-element.18.present_ref, f32[384,256]{1,0:T(8,128)S(1)} %bitcast.9, f32[384,256]{1,0:T(8,128)S(1)} %get-tuple-element.21.force_ref, f32[8,16,256]{2,1,0:T(8,128)S(1)} %get-tuple-element.22.arrived_ref, f32[32,256]{1,0:T(8,128)S(1)} %reshape.23.mass_ref, ...), custom_call_target="tpu_custom_call" | custom-call | tf_op jit(solution)/shard_map/pallas_call | solution.py:461
  64.6 0.2 stack_reshape.6
  64.8 0.3 pad_maximum_fusion
  65.1 1.5 %copy.22 = f32[2,2,2,3,8192]{4,0,3,2,1:T(2,128)} copy(f32[2,2,2,3,8192]{4,3,1,0,2:T(4,128)S(1)} %pad_maximum_fusion) | data formatting | bytes 1572864 | tf_op jit(solution)/shard_map/stack | solution.py:483
  66.6 0.0 collective-permute-done
  66.6 0.1 add_multiply_fusion
  66.7 0.7 %copy.23 = f32[2,125,64]{1,2,0:T(8,128)} copy(f32[2,125,64]{2,1,0:T(8,128)S(1)} %add_multiply_fusion) | data formatting | bytes 128000
  (7 shorter events, 0.1 us)
Async XLA Ops:
  0.6 3.7 %copy-start = (s32[8,6]{1,0:T(8,128)S(1)}, s32[8,6]{1,0:T(8,128)}, u32[]{:S(2)}) copy-start(s32[8,6]{1,0:T(8,128)} %param.18) | copy-start | bytes 580
  0.7 0.8 %copy-start.6 = (s32[125,128]{1,0:T(8,128)S(1)}, s32[125,128]{1,0:T(8,128)}, u32[]{:S(2)}) copy-start(s32[125,128]{1,0:T(8,128)} %param.13) | copy-start | bytes 192004
  0.7 0.9 %copy-start.9 = (s32[1,6,192]{2,0,1:T(1,128)S(1)}, s32[1,6,192]{2,0,1:T(1,128)}, u32[]{:S(2)}) copy-start(s32[1,6,192]{2,0,1:T(1,128)} %param.20) | copy-start | bytes 13828
  1.5 0.7 copy-start.10
  1.5 0.9 %copy-start.7 = (f32[2,125,128]{2,0,1:T(2,128)S(1)}, f32[2,125,128]{2,0,1:T(2,128)}, u32[]{:S(2)}) copy-start(f32[2,125,128]{2,0,1:T(2,128)} %param.16) | copy-start | bytes 384004
  1.5 0.8 %copy-start.8 = (f32[8192]{0:T(1024)S(1)}, f32[8192]{0:T(1024)}, u32[]{:S(2)}) copy-start(f32[8192]{0:T(1024)} %param.17) | copy-start | bytes 98308
  4.2 0.9 %copy-start.2 = (f32[384,128]{1,0:T(8,128)S(1)}, f32[384,128]{1,0:T(8,128)}, u32[]{:S(2)}) copy-start(f32[384,128]{1,0:T(8,128)} %constant.24.clone.refs_7_.forward_ref) | copy-start | bytes 589828
  4.3 1.0 %copy-start.1 = (f32[128,384]{1,0:T(8,128)S(1)}, f32[128,384]{1,0:T(8,128)}, u32[]{:S(2)}) copy-start(f32[128,384]{1,0:T(8,128)} %constant.25.clone.refs_8_.backward_ref) | copy-start | bytes 589828
  4.4 0.9 %copy-start.3 = (f32[128,128]{1,0:T(8,128)S(1)}, f32[128,128]{1,0:T(8,128)}, u32[]{:S(2)}) copy-start(f32[128,128]{1,0:T(8,128)} %constant.26.clone.refs_9_.volume_ref) | copy-start | bytes 196612
  4.4 0.9 %copy-start.4 = (f32[9,128]{1,0:T(8,128)S(1)}, f32[9,128]{1,0:T(8,128)}, u32[]{:S(2)}) copy-start(f32[9,128]{1,0:T(8,128)} %jacobian_ref.1) | copy-start | bytes 13828
  4.5 0.8 %copy-start.5 = (f32[128]{0:T(128)S(1)}, f32[128]{0:T(128)}, u32[]{:S(2)}) copy-start(f32[128]{0:T(128)} %param.15) | copy-start | bytes 1540
  52.3 14.3 %collective-permute-start = (f32[2,125,64]{2,1,0:T(8,128)S(1)}, f32[2,125,64]{2,1,0:T(8,128)S(1)}, u32[]{:S(2)}, u32[]{:S(2)}) collective-permute-start(f32[2,125,64]{2,1,0:T(8,128)S(1)} %slice_select_fusion), channel_id=1, source_target_pairs={{0,1},{1,0},{2,3},{3,2},{4,5},{5,4},{6,7},{7,6},{8,9},{9,8},{10,11... | collective-permute-start | bytes 192008 | tf_op jit(solution)/shard_map/ppermute | solution.py:476

commit v3 on v2

--- a/solution.py
+++ b/solution.py
@@ -313,8 +313,13 @@
         sending_ref[p] = block
 
 
-def swap_and_sum(
-    sending_ref, nodal_force_ref, ids_ref, force_ref, arrived_ref, sum_ref, send_sem, recv_sem
+def step(
+    present_ref, earlier_ref, mass_ref, old_terms_ref,
+    ids_ref, border_ids_ref, jacobian_ref, det_ref, moduli_ref, slots_ref, peers_ref,
+    forward_ref, backward_ref, volume_ref,
+    following_ref, terms_ref, other_terms_ref,
+    nodal_ref, along_ref, traction_ref, packed_ref, border_sum_ref,
+    nodal_force_ref, sending_ref, arrived_ref, force_ref, sum_ref, send_sem, recv_sem,
 ):
     domains = sending_ref.shape[0]
     me = lax.axis_index("dom")
@@ -324,7 +329,18 @@
             barrier, inc=1, device_id={"dom": lax.rem(me + offset, domains)},
             device_id_type=pl.DeviceIdType.MESH,
         )
-    pl.semaphore_wait(barrier, domains - 1)
+    sharer = {"event": 1 - lax.axis_index("event")}
+    pl.semaphore_signal(
+        barrier, inc=1, device_id=sharer, device_id_type=pl.DeviceIdType.MESH
+    )
+    terms_ref[...] = old_terms_ref[...]
+    forces(
+        present_ref, ids_ref, border_ids_ref, jacobian_ref, det_ref, moduli_ref, slots_ref,
+        peers_ref, forward_ref, backward_ref, volume_ref,
+        nodal_force_ref, sending_ref, terms_ref,
+        nodal_ref, along_ref, traction_ref, packed_ref, border_sum_ref,
+    )
+    pl.semaphore_wait(barrier, domains)
     copies = []
     for offset in range(1, domains):
         target = lax.rem(me + offset, domains)
@@ -339,6 +355,17 @@
             )
         )
         copies[-1].start()
+    copies.append(
+        pltpu.make_async_remote_copy(
+            src_ref=terms_ref,
+            dst_ref=other_terms_ref,
+            send_sem=send_sem.at[0],
+            recv_sem=recv_sem.at[0],
+            device_id=sharer,
+            device_id_type=pl.DeviceIdType.MESH,
+        )
+    )
+    copies[-1].start()
     arrived_ref[me] = sending_ref[me]
     sum_ref[...] = jnp.zeros_like(sum_ref)
     half = sum_ref.shape[0] // 2
@@ -351,24 +378,9 @@
     force_ref[...] = sum_ref[:half, :] + sum_ref[half:, :]
     for copy in copies:
         copy.wait()
-
-
-def first_step(present_ref, *refs):
-    refs[12][...] = jnp.zeros_like(refs[12])
-    forces(present_ref, *refs)
-
-
-def next_step(
-    present_ref, earlier_ref, old_force_ref, arrived_ref, mass_ref, old_terms_ref,
-    ids_ref, border_ids_ref, jacobian_ref, det_ref, moduli_ref, slots_ref, peers_ref,
-    forward_ref, backward_ref, volume_ref,
-    following_ref, nodal_force_ref, sending_ref, terms_ref, *scratch
-):
-    combine(present_ref, earlier_ref, old_force_ref, arrived_ref, mass_ref, slots_ref, peers_ref, following_ref)
-    terms_ref[...] = old_terms_ref[...]
-    forces(
-        following_ref, ids_ref, border_ids_ref, jacobian_ref, det_ref, moduli_ref, slots_ref, peers_ref,
-        forward_ref, backward_ref, volume_ref, nodal_force_ref, sending_ref, terms_ref, *scratch
+    combine(
+        present_ref, earlier_ref, force_ref, arrived_ref, mass_ref, slots_ref, peers_ref,
+        following_ref,
     )
 
 
@@ -408,77 +420,40 @@
     smem = pl.BlockSpec(memory_space=pltpu.SMEM)
     common_specs = [vmem, vmem, vmem, vmem, vmem, vmem, smem, vmem, vmem, vmem]
     state = jax.ShapeDtypeStruct((12 * rows, WIDE), f32)
-    made = (
-        jax.ShapeDtypeStruct((128, 12 * 128), f32),
-        jax.ShapeDtypeStruct((domains, 16, WIDE), f32),
-        jax.ShapeDtypeStruct((2, 128, 128), f32),
-    )
-    scratch = [
-        pltpu.VMEM((128, 12 * 128), f32),
-        pltpu.VMEM((3 * 128, 12 * 128), f32),
-        pltpu.VMEM((3 * 128, 12 * 128), f32),
-        pltpu.VMEM((32, 12 * 128), f32),
-        pltpu.VMEM((24 * 16, WIDE), f32),
-    ]
-    params = pltpu.CompilerParams(vmem_limit_bytes=50 * 1024 * 1024)
-
-    def exchange(sending, nodal_force):
-        return pl.pallas_call(
-            swap_and_sum,
-            out_shape=(state, jax.ShapeDtypeStruct(sending.shape, sending.dtype)),
-            in_specs=[vmem] * 3,
-            out_specs=(vmem, vmem),
-            scratch_shapes=[
-                pltpu.VMEM((24 * rows, WIDE), f32),
-                pltpu.SemaphoreType.DMA((domains,)),
-                pltpu.SemaphoreType.DMA((domains,)),
-            ],
-            compiler_params=pltpu.CompilerParams(
-                collective_id=0, has_side_effects=True, vmem_limit_bytes=50 * 1024 * 1024
-            ),
-        )(sending, nodal_force, ids)
-
-    nodal_force, sending, terms = pl.pallas_call(
-        first_step,
-        out_shape=made,
-        in_specs=[vmem] + common_specs,
+    blocks = (domains, 16, WIDE)
+    terms = jnp.zeros((2, 128, 128), f32)
+    take_step = pl.pallas_call(
+        step,
+        out_shape=(state,) + (jax.ShapeDtypeStruct(terms.shape, f32),) * 2,
+        in_specs=[vmem] * 4 + common_specs,
         out_specs=(vmem,) * 3,
-        scratch_shapes=scratch,
-        compiler_params=params,
-    )(present, *common)
-    for _ in range(STEPS - 1):
-        force, arrived = exchange(sending, nodal_force)
-        following, nodal_force, sending, terms = pl.pallas_call(
-            next_step,
-            out_shape=(state,) + made,
-            in_specs=[vmem] * 6 + common_specs,
-            out_specs=(vmem,) * 4,
-            scratch_shapes=scratch,
-            compiler_params=params,
-        )(present, earlier, force, arrived, mass, terms, *common)
+        scratch_shapes=[
+            pltpu.VMEM((128, 12 * 128), f32),
+            pltpu.VMEM((3 * 128, 12 * 128), f32),
+            pltpu.VMEM((3 * 128, 12 * 128), f32),
+            pltpu.VMEM((32, 12 * 128), f32),
+            pltpu.VMEM((24 * 16, WIDE), f32),
+            pltpu.VMEM((128, 12 * 128), f32),
+            pltpu.VMEM(blocks, f32),
+            pltpu.VMEM(blocks, f32),
+            pltpu.VMEM((12 * rows, WIDE), f32),
+            pltpu.VMEM((24 * rows, WIDE), f32),
+            pltpu.SemaphoreType.DMA((domains,)),
+            pltpu.SemaphoreType.DMA((domains,)),
+        ],
+        compiler_params=pltpu.CompilerParams(
+            collective_id=0, has_side_effects=True, vmem_limit_bytes=50 * 1024 * 1024
+        ),
+    )
+    for _ in range(STEPS):
+        following, terms, other_terms = take_step(present, earlier, mass, terms, *common)
         earlier, present = present, following
-    force, arrived = exchange(sending, nodal_force)
-    following = pl.pallas_call(
-        combine,
-        out_shape=state,
-        in_specs=[vmem] * 6 + [smem],
-        out_specs=vmem,
-        compiler_params=params,
-    )(present, earlier, force, arrived, mass, slots, peers)
-    earlier, present = present, following
-
-    sharers = lax.axis_size("event")
-    share_width = element_count // sharers
-    spot = lax.axis_index("event")
-    terms = terms[:, :125]
-    if sharers == 2:
-        low, high = terms[:, :, :share_width], terms[:, :, share_width:]
-        theirs = lax.ppermute(jnp.where(spot == 0, high, low), "event", [(0, 1), (1, 0)])
-        summed = jnp.where(spot == 0, low, high) + theirs
-    else:
-        summed = lax.dynamic_slice_in_dim(
-            lax.psum(terms, "event"), spot * share_width, share_width, 2
-        )
+
+    share_width = element_count // lax.axis_size("event")
+    both = (terms + other_terms)[:, :125]
+    summed = jnp.where(
+        lax.axis_index("event") == 0, both[:, :, :share_width], both[:, :, share_width:]
+    )
     sensitivity = kernel_weight * time_step * summed
     next_wavefields = jnp.stack(
         [present.reshape(events, 2, 3, point_count), earlier.reshape(events, 2, 3, point_count)],

time: 67.7 us -> 61.9 us (0.914)
  Pallas kernels: 58.9 us -> 52.5 us
  local copies, waits for them, and re-layouts: 7 us -> 7.8 us
    pallas_call x5 -> x2, Pallas kernels: 58.9 us -> 52.5 us  [per_device(): take_step(present, earlier, mass, terms, *common)]
    unnamed x25, local copies, waits for them, and re-layouts: 3.95 us -> 4.79 us
  transfers between devices with their start and end apart: 1 -> 0, of which waited for: 0 -> 0; matrix products, arithmetic and copies ran while one was open for 3% -> 0% of each run, Pallas kernels for 18% -> 0%
where the time goes in v3:
time: 61.9 us; the launch traced here: 61.6 us
  Pallas kernels  52.5 us (85%)
  local copies, waits for them, and re-layouts  7.8 us (13%)
  between operations  0.86 us (1%)
    pallas_call x2, Pallas kernels, per_device(): take_step(present, earlier, mass, terms, *common)  52.5 us
    unnamed x25, local copies, waits for them, and re-layouts  4.79 us
    another operation x3, local copies, waits for them, and re-layouts, per_device(): jnp.stack([present.reshape(events, 2, 3, point_count), earlier.reshape(ev...  1.92 us

profile of v3, /device:TPU:0, one launch (start us, length us, event | category | flops | bytes accessed | tf_op | source)
XLA Modules:
  0.0 61.6 jit_solution(11453260052722207154)
XLA Ops:
  0.6 0.0 copy-start
  0.6 0.8 %fusion.2 = (s32[32,32]{1,0:T(8,128)S(1)}, s32[32,32]{1,0:T(8,128)S(1)}, s32[32,32]{1,0:T(8,128)S(1)}, s32[32,32]{1,0:T(8,128)S(1)}) fusion(s32[125,128]{1,0:T(8,128)} %param.13), kind=kLoop, calls=%fused_computation.9 | loop fusion | bytes 131072 | tf_op jit(solution)/shard_map/slice | solution.py:417
  1.4 0.1 pad_add_fusion.border_ids_ref
  1.5 0.0 copy-done
  1.5 1.6 %copy.20 = f32[2,12,8192]{2,1,0:T(8,128)S(1)} copy(f32[2,12,8192]{2,0,1:T(2,128)} %param.12) | data formatting | bytes 1572864 | tf_op args[0]
  3.1 0.2 reshape.20
  3.3 0.0 copy-start.7
  3.3 0.1 fusion.1
  3.4 0.8 %copy-done.7 = f32[2,125,128]{2,0,1:T(2,128)S(1)} copy-done((f32[2,125,128]{2,0,1:T(2,128)S(1)}, f32[2,125,128]{2,0,1:T(2,128)}, u32[]{:S(2)}) %copy-start.7) | copy-done | bytes 128024
  4.3 0.0 copy-start.6
  4.3 0.0 copy-start.8
  4.3 0.0 copy-start.9
  4.3 0.0 copy-start.10
  4.3 0.0 copy-start.2
  4.3 0.8 %copy-done.6 = s32[125,128]{1,0:T(8,128)S(1)} copy-done((s32[125,128]{1,0:T(8,128)S(1)}, s32[125,128]{1,0:T(8,128)}, u32[]{:S(2)}) %copy-start.6) | copy-done | bytes 64024
  5.1 0.0 copy-start.1
  5.1 0.0 copy-done.8
  5.1 0.0 copy-done.9
  5.1 0.0 copy-done.10
  5.2 0.1 bitcast_select_fusion
  5.2 0.0 copy-start.3
  5.2 0.0 copy-start.4
  5.3 0.0 copy-start.5
  5.3 0.0 copy-done.2
  5.3 0.7 %copy-done.1 = f32[384,128]{1,0:T(8,128)S(1)} copy-done((f32[384,128]{1,0:T(8,128)S(1)}, f32[384,128]{1,0:T(8,128)}, u32[]{:S(2)}) %copy-start.1) | copy-done | bytes 196632
  6.0 0.1 copy-done.3
  6.1 0.0 copy-done.4
  6.1 0.0 copy-done.5
  6.1 26.4 %shard_map.131 = (f32[384,256]{1,0:T(8,128)S(1)}, f32[2,128,128]{2,1,0:T(8,128)S(1)}, f32[2,128,128]{2,1,0:T(8,128)}) custom-call(f32[384,256]{1,0:T(8,128)S(1)} %bitcast.7, f32[384,256]{1,0:T(8,128)S(1)} %bitcast.9, f32[32,256]{1,0:T(8,128)S(1)} %reshape.21.mass_ref, f32[2,128,128]{2,1,0:T(8,128)S(1)} %broadcast_in_dim.8.old_terms_ref, ...), custom_call_target="tpu_custom_call" | custom-call | tf_op jit(solution)/shard_map/pallas_call | solution.py:449
  32.6 26.0 %shard_map.132 = (f32[384,256]{1,0:T(8,128)S(1)}, f32[2,128,128]{2,1,0:T(8,128)S(1)}, f32[2,128,128]{2,1,0:T(8,128)S(1)}) custom-call(f32[384,256]{1,0:T(8,128)S(1)} %get-tuple-element.7.present_ref, f32[384,256]{1,0:T(8,128)S(1)} %bitcast.8, f32[32,256]{1,0:T(8,128)S(1)} %reshape.21.mass_ref, f32[2,128,128]{2,1,0:T(8,128)S(1)} %get-tuple-element.8.old_terms_ref, ...), custom_call_target="tpu_custom_call" | custom-call | tf_op jit(solution)/shard_map/pallas_call | solution.py:449
  58.6 0.1 fusion
  58.7 0.7 %copy.23 = f32[2,125,64]{1,2,0:T(8,128)} copy(f32[2,125,64]{2,1,0:T(8,128)S(1)} %fusion) | data formatting | bytes 128000
  59.4 0.2 stack_reshape.6
  59.7 0.2 stack_reshape.7
  59.9 0.3 pad_maximum_fusion
  60.2 1.5 %copy.22 = f32[2,2,2,3,8192]{4,0,3,2,1:T(2,128)} copy(f32[2,2,2,3,8192]{4,3,1,0,2:T(4,128)S(1)} %pad_maximum_fusion) | data formatting | bytes 1572864 | tf_op jit(solution)/shard_map/stack | solution.py:458
  (9 shorter events, 0.1 us)
Async XLA Ops:
  0.6 0.9 %copy-start = (s32[8,6]{1,0:T(8,128)S(1)}, s32[8,6]{1,0:T(8,128)}, u32[]{:S(2)}) copy-start(s32[8,6]{1,0:T(8,128)} %param.18) | copy-start | bytes 580
  3.3 0.9 %copy-start.7 = (f32[2,125,128]{2,0,1:T(2,128)S(1)}, f32[2,125,128]{2,0,1:T(2,128)}, u32[]{:S(2)}) copy-start(f32[2,125,128]{2,0,1:T(2,128)} %param.16) | copy-start | bytes 384004
  4.3 0.8 %copy-start.6 = (s32[125,128]{1,0:T(8,128)S(1)}, s32[125,128]{1,0:T(8,128)}, u32[]{:S(2)}) copy-start(s32[125,128]{1,0:T(8,128)} %param.13) | copy-start | bytes 192004
  4.3 0.8 %copy-start.8 = (f32[8192]{0:T(1024)S(1)}, f32[8192]{0:T(1024)}, u32[]{:S(2)}) copy-start(f32[8192]{0:T(1024)} %param.17) | copy-start | bytes 98308
  4.3 0.9 %copy-start.9 = (s32[1,6,192]{2,0,1:T(1,128)S(1)}, s32[1,6,192]{2,0,1:T(1,128)}, u32[]{:S(2)}) copy-start(s32[1,6,192]{2,0,1:T(1,128)} %param.20) | copy-start | bytes 13828
  4.3 0.9 %copy-start.10 = (s32[1,6]{1,0:T(1,128)S(1)}, s32[1,6]{1,0:T(1,128)}, u32[]{:S(2)}) copy-start(s32[1,6]{1,0:T(1,128)} %param.19) | copy-start | bytes 76
  4.3 1.0 %copy-start.2 = (f32[128,384]{1,0:T(8,128)S(1)}, f32[128,384]{1,0:T(8,128)}, u32[]{:S(2)}) copy-start(f32[128,384]{1,0:T(8,128)} %constant.26.clone.backward_ref) | copy-start | bytes 589828
  5.1 0.9 %copy-start.1 = (f32[384,128]{1,0:T(8,128)S(1)}, f32[384,128]{1,0:T(8,128)}, u32[]{:S(2)}) copy-start(f32[384,128]{1,0:T(8,128)} %constant.25.clone.forward_ref) | copy-start | bytes 589828
  5.2 0.9 %copy-start.3 = (f32[128,128]{1,0:T(8,128)S(1)}, f32[128,128]{1,0:T(8,128)}, u32[]{:S(2)}) copy-start(f32[128,128]{1,0:T(8,128)} %constant.27.clone.volume_ref) | copy-start | bytes 196612
  5.2 0.9 %copy-start.4 = (f32[9,128]{1,0:T(8,128)S(1)}, f32[9,128]{1,0:T(8,128)}, u32[]{:S(2)}) copy-start(f32[9,128]{1,0:T(8,128)} %jacobian_ref.3) | copy-start | bytes 13828
  5.3 0.9 %copy-start.5 = (f32[128]{0:T(128)S(1)}, f32[128]{0:T(128)}, u32[]{:S(2)}) copy-start(f32[128]{0:T(128)} %param.15) | copy-start | bytes 1540
